TPU v7x, 32 devices: a whole 2x2x4 slice. The times are simulated.
32 devices in a mesh: groups: 2 (over y), tensor: 2 (over core), fsdp: 8 (over z, x).
Axes of the slice: x: 2, y: 2, z: 4, core: 2. Of those that a mesh axis runs over, the one named last changes fastest.
Arguments:
- hidden: bfloat16 [4096, 1792], P(('groups', 'fsdp'), 'tensor'), parts along dimension 0, may hold values from -6 to 6
- grad_out: bfloat16 [4096, 4096], P(('groups', 'fsdp'), 'tensor'), parts along dimension 0, may hold values from -6 to 6
- tile_cols: int32 [14, 16], P('tensor'), may hold values from 0 to 31, as said below
- tile_owner: int32 [14, 16], P('tensor'), may hold values from 0 to 7, as said below
- tile_store: bfloat16 [2, 8, 21, 128, 128], P('tensor', 'fsdp'), may hold values from -0.1875 to 0.1875
Outputs:
- mixed_out: bfloat16 [4096, 4096], P(('groups', 'fsdp'), 'tensor'), parts along dimension 0
- grad_hidden: bfloat16 [4096, 1792], P(('groups', 'fsdp'), 'tensor'), parts along dimension 0
- tile_grads: float32 [4, 8, 21, 128, 128], P(('groups', 'tensor'), 'fsdp'), parts along dimension 0
There are 2 independent parts, one for each index of `groups`. A program takes and returns all parts, laid end to end along the dimension named above; an argument that names none is the same for every part. Nothing has to cross between parts.
Inputs may be any that keep to these rules, and one draw needn't show every extreme that they name: `tile_cols`: each row holds 16 different column tile indices in increasing order. `tile_owner`: among the surviving tiles of each aligned block of 7 row tiles (the rows of one tensor index), no fsdp index owns more than 21, and one owns exactly 21.
All inputs are finite; a program needn't handle non-finite values.
Results may differ from a plain program's by a relative error of at most 0.0051.
Values may be sent and summed in bfloat16 or wider, within the bound.
A program may use at most 128 MiB of HBM per device.

v0:
```python
import jax
import jax.numpy as jnp
from jax import lax
from jax.sharding import PartitionSpec as P


def slot_tables(owners, owner_count, capacity):
    number = owners.shape[0]
    tile_ids = jnp.arange(number, dtype=jnp.int32)
    labels = jnp.arange(owner_count, dtype=jnp.int32)
    onehot = (owners[:, None] == labels[None, :]).astype(jnp.int32)
    ranking = jnp.sum((jnp.cumsum(onehot, axis=0) - 1) * onehot, axis=1)
    slot_index = jnp.arange(capacity, dtype=jnp.int32)
    matched = (owners[None, None, :] == labels[:, None, None]) & (
        ranking[None, None, :] == slot_index[None, :, None]
    )
    slot_ids = jnp.sum(jnp.where(matched, tile_ids[None, None, :], 0), axis=2)
    filled = jnp.any(matched, axis=2)
    return (ranking, slot_ids, filled)


def shards(hidden, grad_out, tile_cols, tile_owner, tile_store):
    fsdp_size = lax.axis_size("fsdp")
    tok_rows = hidden.shape[0]
    row_tiles = tile_cols.shape[0]
    keep_count = tile_cols.shape[1]
    capacity = tile_store.shape[2]
    tile_width = tile_store.shape[3]
    col_tiles = 2 * keep_count
    grad_scale = float(tok_rows * fsdp_size) ** (-0.5)
    owner_flat = tile_owner.reshape(-1)
    ranking, slot_ids, filled = slot_tables(owner_flat, fsdp_size, capacity)
    gathered = lax.all_gather(tile_store, "fsdp", axis=1, tiled=True)
    flat_store = gathered.reshape(fsdp_size * capacity, tile_width, tile_width)
    weights = jnp.take(flat_store, owner_flat * capacity + ranking, axis=0).reshape(
        row_tiles, keep_count, tile_width, tile_width
    )
    hid_tiles = hidden.reshape(tok_rows, row_tiles, tile_width)
    col_hot = (
        tile_cols[:, :, None] == jnp.arange(col_tiles, dtype=jnp.int32)[None, None, :]
    ).astype(jnp.bfloat16)
    dense = jnp.einsum("rkab,rkc->racb", weights, col_hot, preferred_element_type=jnp.bfloat16)
    dense = dense.reshape(row_tiles * tile_width, col_tiles * tile_width)
    partial_sum = jnp.dot(hidden, dense, preferred_element_type=jnp.float32)
    summed = lax.psum_scatter(
        partial_sum.astype(jnp.bfloat16), "tensor", scatter_dimension=1, tiled=True
    )
    columns = lax.all_gather(grad_out, "tensor", axis=1, tiled=True)
    col_blocks = columns.reshape(tok_rows, col_tiles, tile_width)
    input_parts = []
    weight_parts = []
    for row_tile in range(row_tiles):
        chosen = jnp.take(col_blocks, tile_cols[row_tile], axis=1)
        input_parts.append(
            jnp.einsum("tkb,kab->ta", chosen, weights[row_tile], preferred_element_type=jnp.float32)
        )
        local_term = jnp.einsum(
            "ta,tkb->kab", hid_tiles[:, row_tile], chosen, preferred_element_type=jnp.float32
        )
        weight_parts.append((local_term * grad_scale).astype(jnp.bfloat16))
    grad_hidden = jnp.concatenate(input_parts, axis=1).astype(jnp.bfloat16)
    pieces = jnp.concatenate(weight_parts, axis=0)
    outgoing = jnp.take(pieces, slot_ids.reshape(-1), axis=0)
    outgoing = jnp.where(filled.reshape(-1)[:, None, None], outgoing, jnp.zeros_like(outgoing))
    outgoing = outgoing.reshape(fsdp_size, capacity, tile_width, tile_width)
    owned_sum = jnp.sum(
        lax.all_to_all(outgoing, "fsdp", split_axis=0, concat_axis=0, tiled=True).astype(
            jnp.float32
        ),
        axis=0,
    )
    grad_hidden, tile_grads = (
        grad_hidden,
        owned_sum.reshape(1, 1, capacity, tile_width, tile_width),
    )
    return (summed, grad_hidden, tile_grads)


def solution(mesh):
    placed = (
        P(("groups", "fsdp"), "tensor"),
        P(("groups", "fsdp"), "tensor"),
        P("tensor", None),
        P("tensor", None),
        P("tensor", "fsdp", None, None, None),
    )
    return jax.shard_map(
        shards,
        mesh=mesh,
        in_specs=placed,
        out_specs=(
            P(("groups", "fsdp"), "tensor"),
            P(("groups", "fsdp"), "tensor"),
            P(("groups", "tensor"), "fsdp", None, None, None),
        ),
        check_vma=False,
    )
```

profile of v0, /device:TPU:0, one launch (start us, length us, event | category | flops | bytes accessed | tf_op | source)
XLA Modules:
  0.0 245.4 jit_solution(4261841941090821633)
XLA Ops:
  7.2 2.3 copy.122
  13.2 10.2 %all-gather.5.cloned.1.call-done = bf16[256,4096]{0,1:T(8,128)(2,1)} async-done(((bf16[256,2048]{0,1:T(8,128)(2,1)}), bf16[256,4096]{0,1:T(8,128)(2,1)}) %all-gather.5.cloned.1.call-update) | async-done | bytes 2097168 | tf_op jit(solution)/shard_map/all_gather | solution.py:48
  23.5 3.2 %copy.123 = bf16[256,32,128]{2,0,1:T(8,128)(2,1)S(1)} copy(bf16[256,32,128]{0,2,1:T(8,128)(2,1)} %bitcast.198) | data formatting | bytes 4194304 | tf_op jit(solution)/shard_map/reshape | solution.py:49
  26.7 1.7 gather_fusion.2
  28.3 1.6 gather_fusion.3
  30.0 1.6 gather_fusion.4
  31.6 1.7 gather_fusion.5
  33.3 1.7 gather_fusion.6
  35.0 1.6 gather_fusion.7
  37.4 3.0 %fusion.32 = bf16[112,128,128]{1,2,0:T(8,128)(2,1)} fusion(bf16[16,256,128]{2,1,0:T(8,128)(2,1)} %gather_fusion.2, pred[16]{0:T(512)(128)(4,1)S(1)} %get-tuple-element.44, bf16[256,7,128]{0,2,1:T(8,128)(2,1)} %bitcast.200), kind=kOutput, calls=%fused_computation.48 | convolution fusion | flops 135266304 | bytes 1638416 | tf_op jit(solution)/shard_map/ta,tkb->kab/dot_general | solution.py:57
  40.4 2.9 %fusion.30 = bf16[112,128,128]{1,2,0:T(8,128)(2,1)} fusion(bf16[112,128,128]{1,2,0:T(8,128)(2,1)} %fusion.32, bf16[16,256,128]{2,1,0:T(8,128)(2,1)} %gather_fusion.3, pred[16]{0:T(512)(128)(4,1)S(1)} %get-tuple-element.42, bf16[256,7,128]{0,2,1:T(8,128)(2,1)} %bitcast.201), kind=kOutput, calls=%fused_computation.46 | convolution fusion | flops 135266304 | bytes 1638416 | tf_op jit(solution)/shard_map/ta,tkb->kab/dot_general | solution.py:57
  43.3 1.6 fusion.28
  44.9 1.6 fusion.26
  46.5 1.6 fusion.24
  48.1 1.7 fusion.22
  49.8 1.6 fusion.20
  51.4 9.8 %gather_fusion.1 = bf16[168,128,128]{1,2,0:T(8,128)(2,1)} fusion(bf16[112,128,128]{1,2,0:T(8,128)(2,1)} %fusion.20, s32[1024]{0:T(1024)S(1)} %pad_clamp_fusion), kind=kCustom, calls=%fused_computation.8 | custom fusion | bytes 11010720 | tf_op jit(solution)/shard_map/jit(_take)/gather | solution.py:63
  61.2 6.3 %select_select_fusion = bf16[8,21,128,128]{2,3,1,0:T(8,128)(2,1)} fusion(bf16[8,21,128,128]{2,3,1,0:T(8,128)(2,1)} %bitcast.194, pred[8,21]{1,0:T(8,128)(4,1)S(1)} %copy.131, pred[8,21]{1,0:T(8,128)(4,1)S(1)} %copy.130), kind=kLoop, calls=%fused_computation.13 | loop fusion | flops 5505024 | bytes 11010384 | tf_op jit(solution)/shard_map/jit(_where)/select_n | solution.py:64
  67.5 5.8 %all-to-all-start = ((bf16[8,21,128,128]{2,3,1,0:T(8,128)(2,1)}), bf16[8,21,128,128]{2,3,1,0:T(8,128)(2,1)}, u32[]{:S(2)}, u32[]{:S(2)}) async-start(bf16[8,21,128,128]{2,3,1,0:T(8,128)(2,1)} %select_select_fusion), calls=%async_computation.1 | async-start | bytes 11010048 | tf_op jit(solution)/shard_map/all_to_all | solution.py:67
  73.7 85.9 %all-gather.3.cloned.1.call-done = bf16[1,8,21,128,128]{4,3,2,0,1:T(8,128)(2,1)} async-done(((bf16[1,1,21,128,128]{4,3,2,0,1:T(8,128)(2,1)}), bf16[1,8,21,128,128]{4,3,2,0,1:T(8,128)(2,1)}) %all-gather.3.cloned.1.call-update) | async-done | bytes 5505040 | tf_op jit(solution)/shard_map/all_gather | solution.py:33
  159.6 5.4 %gather_fusion = bf16[112,128,128]{2,1,0:T(8,128)(2,1)} fusion(bf16[168,128,128]{2,1,0:T(8,128)(2,1)} %bitcast.197, s32[1024]{0:T(1024)S(1)} %pad_clamp_fusion.8), kind=kCustom, calls=%fused_computation.7 | custom fusion | bytes 7340480 | tf_op jit(solution)/shard_map/jit(_take)/gather | solution.py:35
  165.1 5.1 %fusion.9 = bf16[7,32,128,128]{3,1,2,0:T(8,128)(2,1)S(1)} fusion(bf16[7,16,128,128]{3,2,1,0:T(8,128)(2,1)} %bitcast.193, pred[7,16]{1,0:T(8,128)(4,1)S(1)} %compare_and_fusion.1, s32[7,16]{1,0:T(8,128)S(1)} %copy-done.12), kind=kOutput, calls=%fused_computation.17 | convolution fusion | flops 119279104 | bytes 11010608 | tf_op jit(solution)/shard_map/rkab,rkc->racb/dot_general | solution.py:42
  170.2 9.1 %fusion.6 = bf16[256,4096]{0,1:T(8,128)(2,1)} fusion(bf16[256,896]{1,0:T(8,128)(2,1)S(1)} %copy-done.9, bf16[112,8,32,128]{3,2,1,0:T(8,128)(2,1)S(1)} %bitcast.195), kind=kOutput, calls=%fused_computation.15 | convolution fusion | flops 1880096768 | bytes 9895936 | tf_op jit(solution)/shard_map/dot_general | solution.py:44
  179.4 2.8 %broadcast_select_fusion = bf16[112,128,128]{2,1,0:T(8,128)(2,1)S(1)} fusion(bf16[112,128,128]{2,1,0:T(8,128)(2,1)} %gather_fusion, pred[112]{0:T(512)(128)(4,1)S(1)} %compare_and_fusion.9), kind=kLoop, calls=%fused_computation.18 | loop fusion | flops 1835008 | bytes 7340144 | tf_op jit(solution)/shard_map/jit(_take)/select_n | solution.py:35
  184.6 1.2 fusion.38
  188.2 1.2 fusion.44
  189.4 1.2 fusion.46
  190.6 2.0 copy.149
  192.5 38.8 %all-to-all-done = bf16[8,21,128,128]{2,3,1,0:T(8,128)(2,1)} async-done(((bf16[8,21,128,128]{2,3,1,0:T(8,128)(2,1)}), bf16[8,21,128,128]{2,3,1,0:T(8,128)(2,1)}, u32[]{:S(2)}, u32[]{:S(2)}) %all-to-all-start) | async-done | bytes 5505056 | tf_op jit(solution)/shard_map/all_to_all | solution.py:67
  231.3 3.7 %convert_reduce_fusion = f32[21,128,128]{1,2,0:T(8,128)S(1)} fusion(bf16[8,21,128,128]{2,3,1,0:T(8,128)(2,1)} %all-to-all-done), kind=kLoop, calls=%fused_computation.9 | loop fusion | flops 5160960 | bytes 6881280 | tf_op jit(solution)/shard_map/reduce_sum | solution.py:66
  235.0 1.5 copy.150
  236.6 2.3 copy.148
  (66 shorter events, 9.6 us)
Async XLA Ops:
  7.2 3.2 %copy-start.11 = (s32[7,16]{1,0:T(8,128)S(1)}, s32[7,16]{1,0:T(8,128)}, u32[]{:S(2)}) copy-start(s32[7,16]{1,0:T(8,128)} %param.10) | copy-start | bytes 1348
  7.2 3.2 %copy-start.8 = (bf16[256,896]{1,0:T(8,128)(2,1)S(1)}, bf16[256,896]{1,0:T(8,128)(2,1)}, u32[]{:S(2)}) copy-start(bf16[256,896]{1,0:T(8,128)(2,1)} %param.7) | copy-start | bytes 1376260
  7.2 5.9 %copy-start.12 = (s32[7,16]{1,0:T(8,128)S(1)}, s32[7,16]{1,0:T(8,128)}, u32[]{:S(2)}) copy-start(s32[7,16]{1,0:T(8,128)} %param.9) | copy-start | bytes 1348
  7.2 16.3 %all-gather.5.cloned.1.call-start = ((), (), s32[]{:S(2)}) async-start(), calls=%async_computation.4 | async-start | bytes 3145728 | tf_op jit(solution)/shard_map/all_gather | solution.py:48
  9.6 150.1 %all-gather.3.cloned.1.call-start = ((), (), s32[]{:S(2)}) async-start(), calls=%async_computation.2 | async-start | bytes 6193152 | tf_op jit(solution)/shard_map/all_gather | solution.py:33
  37.4 5.9 %copy-start.4 = (bf16[16,256,128]{2,1,0:T(8,128)(2,1)S(1)}, bf16[16,256,128]{2,1,0:T(8,128)(2,1)}, u32[]{:S(2)}) copy-start(bf16[16,256,128]{2,1,0:T(8,128)(2,1)} %gather_fusion.4) | copy-start | bytes 3145732
  37.4 5.9 %copy-start.10 = (bf16[256,896]{0,1:T(8,128)(2,1)S(1)}, bf16[256,896]{0,1:T(8,128)(2,1)}, u32[]{:S(2)}) copy-start(bf16[256,896]{0,1:T(8,128)(2,1)} %copy.132) | copy-start | bytes 1376260
  37.4 7.5 %copy-start.2 = (bf16[16,256,128]{2,1,0:T(8,128)(2,1)S(1)}, bf16[16,256,128]{2,1,0:T(8,128)(2,1)}, u32[]{:S(2)}) copy-start(bf16[16,256,128]{2,1,0:T(8,128)(2,1)} %gather_fusion.5) | copy-start | bytes 3145732
  40.4 6.1 %copy-start.1 = (bf16[16,256,128]{2,1,0:T(8,128)(2,1)S(1)}, bf16[16,256,128]{2,1,0:T(8,128)(2,1)}, u32[]{:S(2)}) copy-start(bf16[16,256,128]{2,1,0:T(8,128)(2,1)} %gather_fusion.6) | copy-start | bytes 3145732
  43.3 4.8 %copy-start = (bf16[16,256,128]{2,1,0:T(8,128)(2,1)S(1)}, bf16[16,256,128]{2,1,0:T(8,128)(2,1)}, u32[]{:S(2)}) copy-start(bf16[16,256,128]{2,1,0:T(8,128)(2,1)} %gather_fusion.7) | copy-start | bytes 3145732
  67.5 163.8 %all-to-all-start = ((bf16[8,21,128,128]{2,3,1,0:T(8,128)(2,1)}), bf16[8,21,128,128]{2,3,1,0:T(8,128)(2,1)}, u32[]{:S(2)}, u32[]{:S(2)}) async-start(bf16[8,21,128,128]{2,3,1,0:T(8,128)(2,1)} %select_select_fusion), calls=%async_computation.1 | async-start | bytes 11010048 | tf_op jit(solution)/shard_map/all_to_all | solution.py:67
  73.3 163.3 %reduce-scatter.2.cloned.1.call-start = ((), (), s32[]{:S(2)}) async-start(), calls=%async_computation.3 | async-start | bytes 3145728 | tf_op jit(solution)/shard_map/reduce_scatter | solution.py:45
  165.1 5.1 %copy-start.9 = (bf16[256,896]{1,0:T(8,128)(2,1)S(1)}, bf16[256,896]{1,0:T(8,128)(2,1)}, u32[]{:S(2)}) copy-start(bf16[256,896]{1,0:T(8,128)(2,1)} %param.7) | copy-start | bytes 1376260
  179.4 2.8 %copy-start.7 = (bf16[16,256,128]{2,1,0:T(8,128)(2,1)S(1)}, bf16[16,256,128]{2,1,0:T(8,128)(2,1)}, u32[]{:S(2)}) copy-start(bf16[16,256,128]{2,1,0:T(8,128)(2,1)} %gather_fusion.2) | copy-start | bytes 3145732
  179.4 4.0 %copy-start.6 = (bf16[16,256,128]{2,1,0:T(8,128)(2,1)S(1)}, bf16[16,256,128]{2,1,0:T(8,128)(2,1)}, u32[]{:S(2)}) copy-start(bf16[16,256,128]{2,1,0:T(8,128)(2,1)} %gather_fusion.3) | copy-start | bytes 3145732
  182.2 2.4 copy-start.5
  182.2 3.6 %copy-start.3 = (bf16[16,256,128]{2,1,0:T(8,128)(2,1)S(1)}, bf16[16,256,128]{2,1,0:T(8,128)(2,1)}, u32[]{:S(2)}) copy-start(bf16[16,256,128]{2,1,0:T(8,128)(2,1)} %gather_fusion.5) | copy-start | bytes 3145732
Sparse Core Ops, SparseCore 0:
  10.2 13.2 all-gather.4
  25.6 133.9 all-gather.2
  179.5 34.7 reduce-scatter.1
where the time goes:
time: 246 us; the launch traced here: 245 us
  waiting for transfers between devices  136 us (55%)
  local copies, waits for them, and re-layouts  38.8 us (16%)
  matrix products  36.6 us (15%)
  other arithmetic  14.3 us (6%)
  between operations  14 us (6%)
  starting transfers between devices  6.07 us (2%)
    all_gather x1, waiting for transfers between devices, shards(): gathered = lax.all_gather(tile_store, 'fsdp', axis=1, tiled=True)  85.9 us
    all_to_all x1, waiting for transfers between devices, shards(): lax.all_to_all(outgoing, 'fsdp', split_axis=0, concat_axis=0, tiled=True)  38.8 us
    dot_general x7, matrix products, shards(): jnp.einsum('ta,tkb->kab', hid_tiles[:, row_tile], chosen, preferred_eleme...  14 us
    gather x7, local copies, waits for them, and re-layouts, shards(): chosen = jnp.take(col_blocks, tile_cols[row_tile], axis=1)  10.7 us
    all_gather x1, waiting for transfers between devices, shards(): columns = lax.all_gather(grad_out, 'tensor', axis=1, tiled=True)  10.2 us
    gather x1, local copies, waits for them, and re-layouts, shards(): outgoing = jnp.take(pieces, slot_ids.reshape(-1), axis=0)  9.75 us
    dot_general x1, matrix products, shards(): partial_sum = jnp.dot(hidden, dense, preferred_element_type=jnp.float32)  9.14 us
    unnamed x31, local copies, waits for them, and re-layouts  9.12 us
  transfers between devices with their start and end apart: 4, of which 3 were waited for; matrix products, arithmetic and copies ran while one was open for 35% of the time, Pallas kernels for 0%

commit v1 on v0

v1 whole, which is shorter than its diff:
```python
import functools

import jax
import jax.numpy as jnp
from jax import lax
from jax.experimental import pallas as pl
from jax.experimental.pallas import tpu as pltpu
from jax.sharding import PartitionSpec as P

MESH = pl.DeviceIdType.MESH


def index_tables(tile_cols, tile_owner, owner_count, capacity, col_tiles):
    row_tiles, keep = tile_cols.shape
    owners = tile_owner.reshape(-1)
    cols = tile_cols.reshape(-1)
    number = owners.shape[0]
    ids = jnp.arange(number, dtype=jnp.int32)
    earlier = (owners[:, None] == owners[None, :]) & (ids[None, :] < ids[:, None])
    rank = jnp.sum(earlier.astype(jnp.int32), axis=1)
    place = owners * capacity + rank
    slots = owner_count * capacity
    match = place[None, :] == jnp.arange(slots, dtype=jnp.int32)[:, None]
    slot_row = row_tiles + jnp.sum(
        jnp.where(match, ids[None, :] // keep - row_tiles, 0), axis=1)
    slot_col = jnp.sum(jnp.where(match, cols[None, :], 0), axis=1)
    hot = tile_cols[:, :, None] == jnp.arange(col_tiles, dtype=jnp.int32)[None, None, :]
    dense = slots + jnp.sum(
        jnp.where(hot, place.reshape(row_tiles, keep)[:, :, None] - slots, 0), axis=1)
    return jnp.concatenate([slot_row, slot_col, dense.reshape(-1)])


def kernel(cfg, tab, hid_ref, grad_ref, store_ref, mixed_ref, gh_ref, tg_ref,
           hid_t, gbuf, wbuf, pbuf, xrecv, zrecv, block, gh_acc, psend, pown, precv,
           g_sem, ax_sem, ar_sem, al_sem, yx_sem, yr_sem, yl_sem,
           rx_sem, rz_send, rz_recv, p_sem):
    lines, capacity, row_tiles, col_tiles, width, scale, paired = cfg
    owners = 2 * lines
    slots = owners * capacity
    half = width // 2
    last = lines - 1
    me = lax.axis_index("fsdp")
    group = lax.axis_index("groups")
    core = lax.axis_index("tensor")
    z, x = me // 2, lax.rem(me, 2)
    x_dev = {"fsdp": z * 2 + 1 - x}
    y_dev = {"groups": 1 - group}
    up_dev = {"fsdp": me + 2}
    down_dev = {"fsdp": me - 2}
    core_dev = {"tensor": 1 - core}
    own_tiles = grad_ref.shape[1] // width

    barrier = pltpu.get_barrier_semaphore()

    def greet(device):
        pl.semaphore_signal(barrier, inc=1, device_id=device, device_id_type=MESH)

    greet(x_dev)
    greet(y_dev)
    if paired:
        greet(core_dev)

    @pl.when(z < last)
    def _():
        greet(up_dev)

    @pl.when(z > 0)
    def _():
        greet(down_dev)

    for h in range(2):
        wbuf[h, pl.ds(me * capacity, capacity)] = store_ref[:, h * half:(h + 1) * half, :]
        wbuf[h, slots] = jnp.zeros((half, width), wbuf.dtype)
    first = core * own_tiles if paired else 0
    for c in range(own_tiles):
        gbuf[first + c] = grad_ref[:, c * width:(c + 1) * width]

    peers = (3 if paired else 2) + jnp.where(z < last, 1, 0) + jnp.where(z > 0, 1, 0)
    pl.semaphore_wait(barrier, peers)

    sent = []

    def copy(src, dst, send, recv, device):
        return pltpu.make_async_remote_copy(
            src_ref=src, dst_ref=dst, send_sem=send, recv_sem=recv,
            device_id=device, device_id_type=MESH)

    def start(cond, desc):
        if cond is None:
            desc.start()
        else:
            @pl.when(cond)
            def _():
                desc.start()
        sent.append((cond, desc))

    def wait_recv(cond, desc):
        if cond is None:
            desc.wait_recv()
        else:
            @pl.when(cond)
            def _():
                desc.wait_recv()

    def chunk(owner):
        return wbuf.at[group, pl.ds(owner * capacity, capacity)]

    def other_chunk(owner):
        return wbuf.at[1 - group, pl.ds(owner * capacity, capacity)]

    def pick(b):
        return x if b == 0 else 1 - x

    def up_send(j, b):
        part = chunk((z - j) * 2 + pick(b))
        return ((z < last) & (z >= j),
                copy(part, part, ar_sem.at[0, j, b], ar_sem.at[1, j, b], up_dev))

    def up_recv(j, b):
        part = chunk((z - 1 - j) * 2 + pick(b))
        return (z >= j + 1, copy(part, part, ar_sem.at[0, j, b], ar_sem.at[1, j, b], up_dev))

    def down_send(j, b):
        part = chunk((z + j) * 2 + pick(b))
        return ((z > 0) & (z + j <= last),
                copy(part, part, al_sem.at[0, j, b], al_sem.at[1, j, b], down_dev))

    def down_recv(j, b):
        part = chunk((z + 1 + j) * 2 + pick(b))
        return (z + 1 + j <= last,
                copy(part, part, al_sem.at[0, j, b], al_sem.at[1, j, b], down_dev))

    def y_up(j, b, part):
        piece = part((z - 1 - j) * 2 + pick(b))
        return (z >= j + 1, copy(piece, piece, yr_sem.at[0, j, b], yr_sem.at[1, j, b], y_dev))

    def y_down(j, b, part):
        piece = part((z + 1 + j) * 2 + pick(b))
        return (z + 1 + j <= last,
                copy(piece, piece, yl_sem.at[0, j, b], yl_sem.at[1, j, b], y_dev))

    def y_x(part):
        piece = part(z * 2 + 1 - x)
        return (None, copy(piece, piece, yx_sem.at[0], yx_sem.at[1], y_dev))

    if paired:
        piece = gbuf.at[pl.ds(core * own_tiles, own_tiles)]
        there = gbuf.at[pl.ds((1 - core) * own_tiles, own_tiles)]
        g_copy = copy(piece, piece, g_sem.at[0], g_sem.at[1], core_dev)
        start(None, g_copy)
    start(None, copy(chunk(me), chunk(me), ax_sem.at[0], ax_sem.at[1], x_dev))
    start(*up_send(0, 0))
    start(*down_send(0, 0))

    for r in range(row_tiles):
        hid_t[r] = hid_ref[:, r * width:(r + 1) * width].T
    hid_t[row_tiles] = jnp.zeros(hid_t.shape[1:], hid_t.dtype)

    if paired:
        copy(there, there, g_sem.at[0], g_sem.at[1], core_dev).wait_recv()

    def pieces(owner):
        def body(s, carry):
            at = owner * capacity + s
            left = hid_t[tab[at]]
            right = gbuf[tab[slots + at]]
            term = jnp.dot(left, right, preferred_element_type=jnp.float32)
            pbuf[at] = (term * scale).astype(pbuf.dtype)
            return carry
        lax.fori_loop(0, capacity, body, 0, unroll=3)

    def shard(owner):
        return pbuf.at[pl.ds(owner * capacity, capacity)]

    def target(k):
        value = jnp.int32(0)
        for at in range(lines):
            order = sorted(range(lines), key=lambda t: -abs(t - at))
            value = jnp.where(z == at, order[k], value)
        return value

    def gather_x():
        part = chunk(z * 2 + 1 - x)
        copy(part, part, ax_sem.at[0], ax_sem.at[1], x_dev).wait_recv()
        start(*up_send(0, 1))
        start(*down_send(0, 1))
        start(*y_x(chunk))

    def gather_z(j, b):
        wait_recv(*up_recv(j, b))
        if j + 1 < last:
            start(*up_send(j + 1, b))
        start(*y_up(j, b, chunk))
        wait_recv(*down_recv(j, b))
        if j + 1 < last:
            start(*down_send(j + 1, b))
        start(*y_down(j, b, chunk))

    steps = [gather_x]
    for j in range(last):
        for b in range(2):
            steps.append(functools.partial(gather_z, j, b))
    steps = iter(steps)

    def gather_step():
        step = next(steps, None)
        if step is not None:
            step()

    targets = [target(k) for k in range(lines)]
    for k in range(lines):
        owner = targets[k] * 2 + 1 - x
        pieces(owner)
        start(None, copy(shard(owner), xrecv.at[k], rx_sem.at[0, k], rx_sem.at[1, k], x_dev))
    gather_step()
    for k in range(lines):
        pieces(targets[k] * 2 + x)
        if k >= lines - 2:
            gather_step()

    def add_up(k):
        goal = targets[k]
        base = (goal * 2 + x) * capacity
        copy(xrecv.at[k], xrecv.at[k], rx_sem.at[0, k], rx_sem.at[1, k], x_dev).wait_recv()
        through = ((goal > z) & (z > 0)) | ((goal < z) & (z < last))

        @pl.when(through)
        def _():
            copy(zrecv.at[goal], zrecv.at[goal], rz_send.at[k], rz_recv.at[goal],
                 x_dev).wait_recv()

            def body(s, carry):
                total = (pbuf[base + s].astype(jnp.float32) + xrecv[k, s].astype(jnp.float32)
                         + zrecv[goal, s].astype(jnp.float32))
                pbuf[base + s] = total.astype(pbuf.dtype)
                return carry
            lax.fori_loop(0, capacity, body, 0)

        @pl.when(jnp.logical_not(through))
        def _():
            def body(s, carry):
                total = pbuf[base + s].astype(jnp.float32) + xrecv[k, s].astype(jnp.float32)
                pbuf[base + s] = total.astype(pbuf.dtype)
                return carry
            lax.fori_loop(0, capacity, body, 0)

        source = pbuf.at[pl.ds(base, capacity)]
        start(goal > z, copy(source, zrecv.at[goal], rz_send.at[k], rz_recv.at[goal], up_dev))
        land = jnp.where(goal == z - 1, lines, goal)
        start(goal < z, copy(source, zrecv.at[land], rz_send.at[k], rz_recv.at[land], down_dev))

    def finish():
        k = last
        base = me * capacity
        copy(xrecv.at[k], xrecv.at[k], rx_sem.at[0, k], rx_sem.at[1, k], x_dev).wait_recv()

        def body(s, carry):
            tg_ref[s] = pbuf[base + s].astype(jnp.float32) + xrecv[k, s].astype(jnp.float32)
            return carry
        lax.fori_loop(0, capacity, body, 0)

        for cond, slot in ((z > 0, z), (z < last, lines)):
            @pl.when(cond)
            def _():
                copy(zrecv.at[slot], zrecv.at[slot], rz_send.at[k], rz_recv.at[slot],
                     x_dev).wait_recv()

                def more(s, carry):
                    tg_ref[s] = tg_ref[s] + zrecv[slot, s].astype(jnp.float32)
                    return carry
                lax.fori_loop(0, capacity, more, 0)

    for k in range(last):
        gather_step()
        add_up(k)
        gather_step()
    for step in steps:
        step()

    wait_recv(*y_x(other_chunk))
    for j in range(last):
        for b in range(2):
            wait_recv(*y_up(j, b, other_chunk))
            wait_recv(*y_down(j, b, other_chunk))

    gh_acc[...] = jnp.zeros_like(gh_acc)

    def products(c0):
        for r in range(row_tiles):
            for q in range(2):
                at = tab[2 * slots + r * col_tiles + c0 + q]
                for h in range(2):
                    block[r * width + h * half:r * width + (h + 1) * half,
                          q * width:(q + 1) * width] = wbuf[h, at]
        dense = block[...]
        cot = jnp.concatenate([gbuf[c0], gbuf[c0 + 1]], axis=1)
        gh_acc[...] += lax.dot_general(cot, dense, (((1,), (1,)), ((), ())),
                                       preferred_element_type=jnp.float32)
        out = jnp.dot(hid_ref[...], dense, preferred_element_type=jnp.float32)
        return out.astype(jnp.bfloat16)

    pairs = own_tiles // 2
    if paired:
        def partial_copy(i):
            return copy(psend.at[i], precv.at[i], p_sem.at[0, i], p_sem.at[1, i], core_dev)

        def away(i, carry):
            psend[i] = products((1 - core) * own_tiles + 2 * i)
            partial_copy(i).start()
            return carry
        lax.fori_loop(0, pairs, away, 0)

        def home(i, carry):
            pown[i] = products(core * own_tiles + 2 * i)
            return carry
        lax.fori_loop(0, pairs, home, 0)
        gh_ref[...] = gh_acc[...].astype(gh_ref.dtype)
        for i in range(pairs):
            partial_copy(i).wait()
            mixed_ref[:, 2 * i * width:2 * (i + 1) * width] = (
                pown[i].astype(jnp.float32) + precv[i].astype(jnp.float32)
            ).astype(mixed_ref.dtype)
    else:
        for i in range(pairs):
            mixed_ref[:, 2 * i * width:2 * (i + 1) * width] = products(2 * i)
        gh_ref[...] = gh_acc[...].astype(gh_ref.dtype)

    finish()
    for cond, desc in sent:
        if cond is None:
            desc.wait_send()
        else:
            pl.when(cond)(desc.wait_send)


def shards(hidden, grad_out, tile_cols, tile_owner, tile_store):
    owners = lax.axis_size("fsdp")
    paired = lax.axis_size("tensor") == 2
    tokens = hidden.shape[0]
    row_tiles, keep = tile_cols.shape
    capacity, width = tile_store.shape[2:4]
    col_tiles = 2 * keep
    lines = owners // 2
    half = width // 2
    slots = owners * capacity
    scale = float(tokens * owners) ** (-0.5)
    tables = index_tables(tile_cols, tile_owner, owners, capacity, col_tiles)
    if not paired:
        grad_out = lax.all_gather(grad_out, "tensor", axis=1, tiled=True)
    store = tile_store.reshape(capacity, width, width)
    hops = lines - 1
    pairs = grad_out.shape[1] // width // 2
    few = pairs if paired else 1
    bf16, f32 = jnp.bfloat16, jnp.float32
    dma = pltpu.SemaphoreType.DMA
    vmem = pl.BlockSpec(memory_space=pltpu.VMEM)
    cfg = (lines, capacity, row_tiles, col_tiles, width, scale, paired)
    mixed, gh, tg = pl.pallas_call(
        functools.partial(kernel, cfg),
        out_shape=(
            jax.ShapeDtypeStruct(grad_out.shape, bf16),
            jax.ShapeDtypeStruct(hidden.shape, bf16),
            jax.ShapeDtypeStruct((capacity, width, width), f32),
        ),
        in_specs=[pl.BlockSpec(memory_space=pltpu.SMEM)] + [vmem] * 3,
        out_specs=(vmem,) * 3,
        scratch_shapes=[
            pltpu.VMEM((row_tiles + 1, width, tokens), bf16),
            pltpu.VMEM((col_tiles, tokens, width), bf16),
            pltpu.VMEM((2, slots + 1, half, width), bf16),
            pltpu.VMEM((slots, width, width), bf16),
            pltpu.VMEM((lines, capacity, width, width), bf16),
            pltpu.VMEM((lines + 1, capacity, width, width), bf16),
            pltpu.VMEM((row_tiles * width, 2 * width), bf16),
            pltpu.VMEM(hidden.shape, f32),
            pltpu.VMEM((few, tokens, 2 * width), bf16),
            pltpu.VMEM((few, tokens, 2 * width), bf16),
            pltpu.VMEM((few, tokens, 2 * width), bf16),
            dma((2,)), dma((2,)), dma((2, hops, 2)), dma((2, hops, 2)),
            dma((2,)), dma((2, hops, 2)), dma((2, hops, 2)),
            dma((2, lines)), dma((lines,)), dma((lines + 1,)), dma((2, few)),
        ],
        compiler_params=pltpu.CompilerParams(
            collective_id=0, has_side_effects=True, vmem_limit_bytes=48 * 1024 * 1024),
    )(tables, hidden, grad_out, store)
    if not paired:
        mixed = lax.psum_scatter(mixed, "tensor", scatter_dimension=1, tiled=True)
    return mixed, gh, tg.reshape(1, 1, capacity, width, width)


def solution(mesh):
    placed = (
        P(("groups", "fsdp"), "tensor"),
        P(("groups", "fsdp"), "tensor"),
        P("tensor", None),
        P("tensor", None),
        P("tensor", "fsdp", None, None, None),
    )
    return jax.shard_map(
        shards,
        mesh=mesh,
        in_specs=placed,
        out_specs=(
            P(("groups", "fsdp"), "tensor"),
            P(("groups", "fsdp"), "tensor"),
            P(("groups", "tensor"), "fsdp", None, None, None),
        ),
        check_vma=False,
    )
```

time: 246 us -> 86.3 us (0.35)
  waiting for transfers between devices: 136 us -> 0 us
  Pallas kernels: 0 us -> 75.5 us
  matrix products: 36.6 us -> 0 us
  local copies, waits for them, and re-layouts: 38.8 us -> 7.86 us
  between operations: 14 us -> 0.67 us
  other arithmetic: 14.3 us -> 1.9 us
  starting transfers between devices: 6.07 us -> 0 us
    all_gather x2 -> x0, waiting for transfers between devices: 96.2 us -> none  [the longest x1 85.9 us: shards(): gathered = lax.all_gather(tile_store, 'fsdp', axis=1, tiled=True)]
    pallas_call x0 -> x1, Pallas kernels: none -> 75.5 us  [shards(): pl.pallas_call(functools.partial(kernel, cfg), out_shape=(jax.ShapeDtypeS...]
    all_to_all x1 -> x0, waiting for transfers between devices: 38.8 us -> none  [shards(): lax.all_to_all(outgoing, 'fsdp', split_axis=0, concat_axis=0, tiled=True)]
    dot_general x16 -> x0, matrix products: 36.6 us -> none  [the longest x7 14 us: shards(): jnp.einsum('ta,tkb->kab', hid_tiles[:, row_tile], chosen, preferred_eleme...]
    gather x9 -> x0, local copies, waits for them, and re-layouts: 25.8 us -> none  [the longest x7 10.7 us: shards(): chosen = jnp.take(col_blocks, tile_cols[row_tile], axis=1)]
    select_n x4 -> x0, other arithmetic: 9.15 us -> none  [the longest x1 6.34 us: shards(): jnp.where(filled.reshape(-1)[:, None, None], outgoing, jnp.zeros_like(out...]
    all_to_all x1 -> x0, starting transfers between devices: 5.77 us -> none  [shards(): lax.all_to_all(outgoing, 'fsdp', split_axis=0, concat_axis=0, tiled=True)]
    reduce_sum x3, other arithmetic: 4.32 us -> 1.11 us  [the longest x1 0.79 us: index_tables(): jnp.sum(jnp.where(hot, place.reshape(row_tiles, keep)[:, :, None] - slots...]
  transfers between devices with their start and end apart: 4 -> 0, of which waited for: 3 -> 0; matrix products, arithmetic and copies ran while one was open for 35% -> 0% of each run, Pallas kernels for 0% -> 0%
where the time goes in v1:
time: 86.3 us; the launch traced here: 86 us
  Pallas kernels  75.5 us (87%)
  local copies, waits for them, and re-layouts  7.86 us (9%)
  other arithmetic  1.9 us (2%)
    pallas_call x1, Pallas kernels, shards(): pl.pallas_call(functools.partial(kernel, cfg), out_shape=(jax.ShapeDtypeS...  75.5 us
    unnamed x9, local copies, waits for them, and re-layouts  6.16 us

profile of v1, /device:TPU:0, one launch (start us, length us, event | category | flops | bytes accessed | tf_op | source)
XLA Modules:
  0.0 86.0 jit_solution(1608417227236244301)
XLA Ops:
  0.6 0.8 reshape.74
  1.4 0.2 convert_reduce_fusion
  1.6 0.8 broadcast_in_dim.41
  2.4 0.2 select_reduce_fusion.1
  2.5 0.1 reduce_sum.41
  2.6 0.7 add_add_fusion
  3.3 0.8 select_reduce_fusion.2
  4.1 0.1 add.46
  4.2 0.1 pad_add_fusion.tab
  4.3 0.0 copy-start
  4.3 1.2 %copy-done = bf16[256,2048]{1,0:T(8,128)(2,1)S(1)} copy-done((bf16[256,2048]{1,0:T(8,128)(2,1)S(1)}, bf16[256,2048]{1,0:T(8,128)(2,1)}, u32[]{:S(2)}) %copy-start) | copy-done | bytes 1048600
  5.5 0.0 copy-start.1
  5.5 1.1 %copy-done.1 = bf16[1,1,21,128,128]{4,3,2,1,0:T(8,128)(2,1)S(1)} copy-done((bf16[1,1,21,128,128]{4,3,2,1,0:T(8,128)(2,1)S(1)}, bf16[1,1,21,128,128]{4,3,2,1,0:T(8,128)(2,1)}, u32[]{:S(2)}) %copy-start.1) | copy-done | bytes 688152
  6.6 0.0 copy-start.2
  6.6 1.0 %copy-done.2 = bf16[256,896]{1,0:T(8,128)(2,1)S(1)} copy-done((bf16[256,896]{1,0:T(8,128)(2,1)S(1)}, bf16[256,896]{1,0:T(8,128)(2,1)}, u32[]{:S(2)}) %copy-start.2) | copy-done | bytes 458776
  7.6 75.5 %shard_map.76 = (bf16[256,2048]{1,0:T(8,128)(2,1)S(1)}, bf16[256,896]{1,0:T(8,128)(2,1)S(1)}, f32[21,128,128]{2,1,0:T(8,128)S(1)}) custom-call(s32[560]{0:T(1024)S(1)} %pad_add_fusion.tab, bf16[256,896]{1,0:T(8,128)(2,1)S(1)} %copy-done.2, bf16[256,2048]{1,0:T(8,128)(2,1)S(1)} %copy-done, bf16[21,128,128]{2,1,0:T(8,128)(2,1)S(1)} %bitcast.3), custom_call_target="tpu_custom_call" | custom-call | tf_op jit(solution)/shard_map/pallas_call | solution.py:358
  83.1 1.0 %copy.11 = bf16[256,2048]{1,0:T(8,128)(2,1)} copy(bf16[256,2048]{1,0:T(8,128)(2,1)S(1)} %get-tuple-element.16) | data formatting | bytes 2097152
  84.1 0.8 copy.12
  84.9 1.1 %copy.13 = f32[1,1,21,128,128]{4,3,2,1,0:T(8,128)} copy(f32[1,1,21,128,128]{4,3,2,1,0:T(8,128)S(1)} %bitcast.2) | data formatting | bytes 2752512
  (3 shorter events, 0.0 us)
Async XLA Ops:
  4.3 1.2 %copy-start = (bf16[256,2048]{1,0:T(8,128)(2,1)S(1)}, bf16[256,2048]{1,0:T(8,128)(2,1)}, u32[]{:S(2)}) copy-start(bf16[256,2048]{1,0:T(8,128)(2,1)} %grad_ref.1) | copy-start | bytes 3145732
  5.5 1.1 %copy-start.1 = (bf16[1,1,21,128,128]{4,3,2,1,0:T(8,128)(2,1)S(1)}, bf16[1,1,21,128,128]{4,3,2,1,0:T(8,128)(2,1)}, u32[]{:S(2)}) copy-start(bf16[1,1,21,128,128]{4,3,2,1,0:T(8,128)(2,1)} %param.9) | copy-start | bytes 2064388
  6.6 1.0 %copy-start.2 = (bf16[256,896]{1,0:T(8,128)(2,1)S(1)}, bf16[256,896]{1,0:T(8,128)(2,1)}, u32[]{:S(2)}) copy-start(bf16[256,896]{1,0:T(8,128)(2,1)} %hid_ref.1) | copy-start | bytes 1376260

commit v2 on v1

--- a/solution.py
+++ b/solution.py
@@ -21,20 +21,21 @@
     place = owners * capacity + rank
     slots = owner_count * capacity
     match = place[None, :] == jnp.arange(slots, dtype=jnp.int32)[:, None]
-    slot_row = row_tiles + jnp.sum(
-        jnp.where(match, ids[None, :] // keep - row_tiles, 0), axis=1)
-    slot_col = jnp.sum(jnp.where(match, cols[None, :], 0), axis=1)
+    zero_tile = row_tiles * col_tiles
+    tile = ids // keep * col_tiles + cols
+    slot_tile = zero_tile + jnp.sum(jnp.where(match, tile[None, :] - zero_tile, 0), axis=1)
     hot = tile_cols[:, :, None] == jnp.arange(col_tiles, dtype=jnp.int32)[None, None, :]
     dense = slots + jnp.sum(
         jnp.where(hot, place.reshape(row_tiles, keep)[:, :, None] - slots, 0), axis=1)
-    return jnp.concatenate([slot_row, slot_col, dense.reshape(-1)])
-
-
-def kernel(cfg, tab, hid_ref, grad_ref, store_ref, mixed_ref, gh_ref, tg_ref,
-           hid_t, gbuf, wbuf, pbuf, xrecv, zrecv, block, gh_acc, psend, pown, precv,
+    return jnp.concatenate([slot_tile, dense.reshape(-1)])
+
+
+def kernel(cfg, tab, hid_hbm, grad_hbm, store_hbm, mixed_ref, gh_ref, tg_ref,
+           hid, hid_t, gfull, wbuf, dmat, pbuf, xrecv, zrecv, block, gh_acc,
+           psend, pown, precv, in_sem,
            g_sem, ax_sem, ar_sem, al_sem, yx_sem, yr_sem, yl_sem,
            rx_sem, rz_send, rz_recv, p_sem):
-    lines, capacity, row_tiles, col_tiles, width, scale, paired = cfg
+    lines, capacity, row_tiles, col_tiles, width, scale, paired, subs = cfg
     owners = 2 * lines
     slots = owners * capacity
     half = width // 2
@@ -48,8 +49,18 @@
     up_dev = {"fsdp": me + 2}
     down_dev = {"fsdp": me - 2}
     core_dev = {"tensor": 1 - core}
-    own_tiles = grad_ref.shape[1] // width
-
+    own_tiles = grad_hbm.shape[1] // width
+    part = capacity // subs
+    first = core if paired else 0
+
+    own_rows = pl.ds(me * capacity, capacity)
+    hid_in = pltpu.make_async_copy(hid_hbm, hid, in_sem.at[0])
+    grad_in = pltpu.make_async_copy(grad_hbm, gfull.at[first], in_sem.at[1])
+    store_in = [pltpu.make_async_copy(store_hbm.at[:, h * half:(h + 1) * half, :],
+                                      wbuf.at[h, own_rows], in_sem.at[2 + h])
+                for h in range(2)]
+    hid_in.start()
+    grad_in.start()
     barrier = pltpu.get_barrier_semaphore()
 
     def greet(device):
@@ -69,11 +80,8 @@
         greet(down_dev)
 
     for h in range(2):
-        wbuf[h, pl.ds(me * capacity, capacity)] = store_ref[:, h * half:(h + 1) * half, :]
         wbuf[h, slots] = jnp.zeros((half, width), wbuf.dtype)
-    first = core * own_tiles if paired else 0
-    for c in range(own_tiles):
-        gbuf[first + c] = grad_ref[:, c * width:(c + 1) * width]
+    dmat[row_tiles * col_tiles] = jnp.zeros((width, width), dmat.dtype)
 
     peers = (3 if paired else 2) + jnp.where(z < last, 1, 0) + jnp.where(z > 0, 1, 0)
     pl.semaphore_wait(barrier, peers)
@@ -143,34 +151,57 @@
         piece = part(z * 2 + 1 - x)
         return (None, copy(piece, piece, yx_sem.at[0], yx_sem.at[1], y_dev))
 
+    mine = store_hbm.at[:, pl.ds(pl.multiple_of(group * half, half), half), :]
+
+    def from_store(cond, sems, device):
+        start(cond, copy(mine, chunk(me), sems[0], sems[1], device))
+
+    from_store(None, (ax_sem.at[0], ax_sem.at[1]), x_dev)
     if paired:
-        piece = gbuf.at[pl.ds(core * own_tiles, own_tiles)]
-        there = gbuf.at[pl.ds((1 - core) * own_tiles, own_tiles)]
-        g_copy = copy(piece, piece, g_sem.at[0], g_sem.at[1], core_dev)
-        start(None, g_copy)
-    start(None, copy(chunk(me), chunk(me), ax_sem.at[0], ax_sem.at[1], x_dev))
-    start(*up_send(0, 0))
-    start(*down_send(0, 0))
-
+        start(None, copy(grad_hbm, gfull.at[core], g_sem.at[0], g_sem.at[1], core_dev))
+    from_store(z < last, (ar_sem.at[0, 0, 0], ar_sem.at[1, 0, 0]), up_dev)
+    from_store(z > 0, (al_sem.at[0, 0, 0], al_sem.at[1, 0, 0]), down_dev)
+    for desc in store_in:
+        desc.start()
+
+    hid_in.wait()
     for r in range(row_tiles):
-        hid_t[r] = hid_ref[:, r * width:(r + 1) * width].T
-    hid_t[row_tiles] = jnp.zeros(hid_t.shape[1:], hid_t.dtype)
-
+        hid_t[r * width:(r + 1) * width] = hid[:, r * width:(r + 1) * width].T
+
+    pairs = own_tiles // 2
+
+    def columns(side, i):
+        return gfull[side, :, pl.ds(pl.multiple_of(2 * i * width, 2 * width), 2 * width)]
+
+    def gradients(side):
+        def body(i, carry):
+            term = jnp.dot(hid_t[...], columns(side, i), preferred_element_type=jnp.float32)
+            term = (term * scale).astype(dmat.dtype)
+            at = side * own_tiles + 2 * i
+            for r in range(row_tiles):
+                for q in range(2):
+                    dmat[r * col_tiles + at + q] = term[r * width:(r + 1) * width,
+                                                        q * width:(q + 1) * width]
+            return carry
+        lax.fori_loop(0, pairs, body, 0)
+
+    grad_in.wait()
+    gradients(first)
     if paired:
+        there = gfull.at[1 - core]
         copy(there, there, g_sem.at[0], g_sem.at[1], core_dev).wait_recv()
-
-    def pieces(owner):
+        gradients(1 - core)
+
+    def pieces(owner, sub):
+        base = owner * capacity + sub * part
+
         def body(s, carry):
-            at = owner * capacity + s
-            left = hid_t[tab[at]]
-            right = gbuf[tab[slots + at]]
-            term = jnp.dot(left, right, preferred_element_type=jnp.float32)
-            pbuf[at] = (term * scale).astype(pbuf.dtype)
+            pbuf[base + s] = dmat[tab[base + s]]
             return carry
-        lax.fori_loop(0, capacity, body, 0, unroll=3)
-
-    def shard(owner):
-        return pbuf.at[pl.ds(owner * capacity, capacity)]
+        lax.fori_loop(0, part, body, 0, unroll=True)
+
+    def shard(owner, sub):
+        return pbuf.at[pl.ds(owner * capacity + sub * part, part)]
 
     def target(k):
         value = jnp.int32(0)
@@ -208,75 +239,94 @@
             step()
 
     targets = [target(k) for k in range(lines)]
+
+    def x_copy(k, sub):
+        owner = targets[k] * 2 + 1 - x
+        i = k * subs + sub
+        return copy(shard(owner, sub), xrecv.at[i], rx_sem.at[0, i], rx_sem.at[1, i], x_dev)
+
     for k in range(lines):
-        owner = targets[k] * 2 + 1 - x
-        pieces(owner)
-        start(None, copy(shard(owner), xrecv.at[k], rx_sem.at[0, k], rx_sem.at[1, k], x_dev))
-    gather_step()
+        for sub in range(subs):
+            pieces(targets[k] * 2 + 1 - x, sub)
+            start(None, x_copy(k, sub))
+        if k == 0:
+            gather_step()
     for k in range(lines):
-        pieces(targets[k] * 2 + x)
-        if k >= lines - 2:
+        for sub in range(subs):
+            pieces(targets[k] * 2 + x, sub)
+        if k == 0:
             gather_step()
 
-    def add_up(k):
+    def arrived(slot, k, sub):
+        copy(zrecv.at[slot, sub], zrecv.at[slot, sub], rz_send.at[k, sub],
+             rz_recv.at[slot, sub], x_dev).wait_recv()
+
+    def add_up(k, sub):
         goal = targets[k]
-        base = (goal * 2 + x) * capacity
-        copy(xrecv.at[k], xrecv.at[k], rx_sem.at[0, k], rx_sem.at[1, k], x_dev).wait_recv()
+        i = k * subs + sub
+        base = (goal * 2 + x) * capacity + sub * part
+        x_copy(k, sub).wait_recv()
         through = ((goal > z) & (z > 0)) | ((goal < z) & (z < last))
 
         @pl.when(through)
         def _():
-            copy(zrecv.at[goal], zrecv.at[goal], rz_send.at[k], rz_recv.at[goal],
-                 x_dev).wait_recv()
+            arrived(goal, k, sub)
 
             def body(s, carry):
-                total = (pbuf[base + s].astype(jnp.float32) + xrecv[k, s].astype(jnp.float32)
-                         + zrecv[goal, s].astype(jnp.float32))
+                total = (pbuf[base + s].astype(jnp.float32) + xrecv[i, s].astype(jnp.float32)
+                         + zrecv[goal, sub, s].astype(jnp.float32))
                 pbuf[base + s] = total.astype(pbuf.dtype)
                 return carry
-            lax.fori_loop(0, capacity, body, 0)
+            lax.fori_loop(0, part, body, 0)
 
         @pl.when(jnp.logical_not(through))
         def _():
             def body(s, carry):
-                total = pbuf[base + s].astype(jnp.float32) + xrecv[k, s].astype(jnp.float32)
+                total = pbuf[base + s].astype(jnp.float32) + xrecv[i, s].astype(jnp.float32)
                 pbuf[base + s] = total.astype(pbuf.dtype)
                 return carry
-            lax.fori_loop(0, capacity, body, 0)
-
-        source = pbuf.at[pl.ds(base, capacity)]
-        start(goal > z, copy(source, zrecv.at[goal], rz_send.at[k], rz_recv.at[goal], up_dev))
+            lax.fori_loop(0, part, body, 0)
+
+        source = pbuf.at[pl.ds(base, part)]
         land = jnp.where(goal == z - 1, lines, goal)
-        start(goal < z, copy(source, zrecv.at[land], rz_send.at[k], rz_recv.at[land], down_dev))
-
-    def finish():
+        start(goal > z, copy(source, zrecv.at[goal, sub], rz_send.at[k, sub],
+                             rz_recv.at[goal, sub], up_dev))
+        start(goal < z, copy(source, zrecv.at[land, sub], rz_send.at[k, sub],
+                             rz_recv.at[land, sub], down_dev))
+
+    def finish(sub):
         k = last
-        base = me * capacity
-        copy(xrecv.at[k], xrecv.at[k], rx_sem.at[0, k], rx_sem.at[1, k], x_dev).wait_recv()
+        i = k * subs + sub
+        base = me * capacity + sub * part
+        x_copy(k, sub).wait_recv()
 
         def body(s, carry):
-            tg_ref[s] = pbuf[base + s].astype(jnp.float32) + xrecv[k, s].astype(jnp.float32)
+            tg_ref[sub * part + s] = (pbuf[base + s].astype(jnp.float32)
+                                      + xrecv[i, s].astype(jnp.float32))
             return carry
-        lax.fori_loop(0, capacity, body, 0)
+        lax.fori_loop(0, part, body, 0)
 
         for cond, slot in ((z > 0, z), (z < last, lines)):
             @pl.when(cond)
             def _():
-                copy(zrecv.at[slot], zrecv.at[slot], rz_send.at[k], rz_recv.at[slot],
-                     x_dev).wait_recv()
+                arrived(slot, k, sub)
 
                 def more(s, carry):
-                    tg_ref[s] = tg_ref[s] + zrecv[slot, s].astype(jnp.float32)
+                    at = sub * part + s
+                    tg_ref[at] = tg_ref[at] + zrecv[slot, sub, s].astype(jnp.float32)
                     return carry
-                lax.fori_loop(0, capacity, more, 0)
+                lax.fori_loop(0, part, more, 0)
 
     for k in range(last):
-        gather_step()
-        add_up(k)
-        gather_step()
+        for sub in range(subs):
+            add_up(k, sub)
+            if sub % 2 == 0:
+                gather_step()
     for step in steps:
         step()
 
+    for desc in store_in:
+        desc.wait()
     wait_recv(*y_x(other_chunk))
     for j in range(last):
         for b in range(2):
@@ -285,33 +335,33 @@
 
     gh_acc[...] = jnp.zeros_like(gh_acc)
 
-    def products(c0):
+    def products(side, i):
+        c0 = side * own_tiles + 2 * i
         for r in range(row_tiles):
             for q in range(2):
-                at = tab[2 * slots + r * col_tiles + c0 + q]
+                at = tab[slots + r * col_tiles + c0 + q]
                 for h in range(2):
                     block[r * width + h * half:r * width + (h + 1) * half,
                           q * width:(q + 1) * width] = wbuf[h, at]
         dense = block[...]
-        cot = jnp.concatenate([gbuf[c0], gbuf[c0 + 1]], axis=1)
+        cot = columns(side, i)
         gh_acc[...] += lax.dot_general(cot, dense, (((1,), (1,)), ((), ())),
                                        preferred_element_type=jnp.float32)
-        out = jnp.dot(hid_ref[...], dense, preferred_element_type=jnp.float32)
+        out = jnp.dot(hid[...], dense, preferred_element_type=jnp.float32)
         return out.astype(jnp.bfloat16)
 
-    pairs = own_tiles // 2
     if paired:
         def partial_copy(i):
             return copy(psend.at[i], precv.at[i], p_sem.at[0, i], p_sem.at[1, i], core_dev)
 
         def away(i, carry):
-            psend[i] = products((1 - core) * own_tiles + 2 * i)
+            psend[i] = products(1 - core, i)
             partial_copy(i).start()
             return carry
         lax.fori_loop(0, pairs, away, 0)
 
         def home(i, carry):
-            pown[i] = products(core * own_tiles + 2 * i)
+            pown[i] = products(core, i)
             return carry
         lax.fori_loop(0, pairs, home, 0)
         gh_ref[...] = gh_acc[...].astype(gh_ref.dtype)
@@ -322,10 +372,11 @@
             ).astype(mixed_ref.dtype)
     else:
         for i in range(pairs):
-            mixed_ref[:, 2 * i * width:2 * (i + 1) * width] = products(2 * i)
+            mixed_ref[:, 2 * i * width:2 * (i + 1) * width] = products(0, i)
         gh_ref[...] = gh_acc[...].astype(gh_ref.dtype)
 
-    finish()
+    for sub in range(subs):
+        finish(sub)
     for cond, desc in sent:
         if cond is None:
             desc.wait_send()
@@ -350,11 +401,14 @@
     store = tile_store.reshape(capacity, width, width)
     hops = lines - 1
     pairs = grad_out.shape[1] // width // 2
+    subs = 3 if capacity % 3 == 0 else 1
+    part = capacity // subs
+    sides = 2 if paired else 1
     few = pairs if paired else 1
     bf16, f32 = jnp.bfloat16, jnp.float32
     dma = pltpu.SemaphoreType.DMA
     vmem = pl.BlockSpec(memory_space=pltpu.VMEM)
-    cfg = (lines, capacity, row_tiles, col_tiles, width, scale, paired)
+    cfg = (lines, capacity, row_tiles, col_tiles, width, scale, paired, subs)
     mixed, gh, tg = pl.pallas_call(
         functools.partial(kernel, cfg),
         out_shape=(
@@ -362,26 +416,28 @@
             jax.ShapeDtypeStruct(hidden.shape, bf16),
             jax.ShapeDtypeStruct((capacity, width, width), f32),
         ),
-        in_specs=[pl.BlockSpec(memory_space=pltpu.SMEM)] + [vmem] * 3,
+        in_specs=[pl.BlockSpec(memory_space=pltpu.SMEM)] + [pl.BlockSpec(memory_space=pl.ANY)] * 3,
         out_specs=(vmem,) * 3,
         scratch_shapes=[
-            pltpu.VMEM((row_tiles + 1, width, tokens), bf16),
-            pltpu.VMEM((col_tiles, tokens, width), bf16),
+            pltpu.VMEM(hidden.shape, bf16),
+            pltpu.VMEM((row_tiles * width, tokens), bf16),
+            pltpu.VMEM((sides,) + grad_out.shape, bf16),
             pltpu.VMEM((2, slots + 1, half, width), bf16),
+            pltpu.VMEM((row_tiles * col_tiles + 1, width, width), bf16),
             pltpu.VMEM((slots, width, width), bf16),
-            pltpu.VMEM((lines, capacity, width, width), bf16),
-            pltpu.VMEM((lines + 1, capacity, width, width), bf16),
+            pltpu.VMEM((lines * subs, part, width, width), bf16),
+            pltpu.VMEM((lines + 1, subs, part, width, width), bf16),
             pltpu.VMEM((row_tiles * width, 2 * width), bf16),
             pltpu.VMEM(hidden.shape, f32),
             pltpu.VMEM((few, tokens, 2 * width), bf16),
             pltpu.VMEM((few, tokens, 2 * width), bf16),
             pltpu.VMEM((few, tokens, 2 * width), bf16),
-            dma((2,)), dma((2,)), dma((2, hops, 2)), dma((2, hops, 2)),
+            dma((4,)), dma((2,)), dma((2,)), dma((2, hops, 2)), dma((2, hops, 2)),
             dma((2,)), dma((2, hops, 2)), dma((2, hops, 2)),
-            dma((2, lines)), dma((lines,)), dma((lines + 1,)), dma((2, few)),
+            dma((2, lines * subs)), dma((lines, subs)), dma((lines + 1, subs)), dma((2, few)),
         ],
         compiler_params=pltpu.CompilerParams(
-            collective_id=0, has_side_effects=True, vmem_limit_bytes=48 * 1024 * 1024),
+            collective_id=0, has_side_effects=True, vmem_limit_bytes=56 * 1024 * 1024),
     )(tables, hidden, grad_out, store)
     if not paired:
         mixed = lax.psum_scatter(mixed, "tensor", scatter_dimension=1, tiled=True)

time: 86.3 us -> 88.5 us (1.025)
  Pallas kernels: 75.5 us -> 79.1 us
  local copies, waits for them, and re-layouts: 7.86 us -> 5.99 us
    pallas_call x1, Pallas kernels: 75.5 us -> 79.1 us  [shards(): pl.pallas_call(functools.partial(kernel, cfg), out_shape=(jax.ShapeDtypeS...]
    unnamed x9 -> x7, local copies, waits for them, and re-layouts: 6.16 us -> 4.29 us
where the time goes in v2:
time: 88.5 us; the launch traced here: 88.2 us
  Pallas kernels  79.1 us (89%)
  local copies, waits for them, and re-layouts  5.99 us (7%)
  other arithmetic  2.45 us (3%)
    pallas_call x1, Pallas kernels, shards(): pl.pallas_call(functools.partial(kernel, cfg), out_shape=(jax.ShapeDtypeS...  79.1 us
    unnamed x7, local copies, waits for them, and re-layouts  4.29 us

profile of v2, /device:TPU:0, one launch (start us, length us, event | category | flops | bytes accessed | tf_op | source)
XLA Modules:
  0.0 88.2 jit_solution(18080767109663107821)
XLA Ops:
  0.6 0.8 reshape.58
  1.4 0.2 convert_reduce_fusion
  1.6 0.8 reshape.59
  2.4 0.1 select_reduce_fusion
  2.5 0.1 reduce_sum.31
  2.6 0.7 add_add_fusion
  3.3 0.8 select_reduce_fusion.1
  4.1 0.1 add.53
  4.1 0.7 pad_add_fusion.tab
  4.8 79.1 %shard_map.76 = (bf16[256,2048]{1,0:T(8,128)(2,1)}, bf16[256,896]{1,0:T(8,128)(2,1)}, f32[21,128,128]{2,1,0:T(8,128)}) custom-call(s32[392]{0:T(512)} %pad_add_fusion.tab, bf16[256,896]{1,0:T(8,128)(2,1)} %hid_hbm.1, bf16[256,2048]{1,0:T(8,128)(2,1)} %grad_hbm.1, bf16[21,128,128]{2,1,0:T(8,128)(2,1)} %bitcast.3), custom_call_target="tpu_custom_call" | custom-call | tf_op jit(solution)/shard_map/pallas_call | solution.py:412
  83.9 0.0 copy-start.1
  83.9 0.0 copy-start
  83.9 2.4 %copy.11 = bf16[256,2048]{1,0:T(8,128)(2,1)} copy(bf16[256,2048]{1,0:T(8,128)(2,1)} %get-tuple-element.14) | data formatting | bytes 2097152
  86.4 0.0 copy-done.1
  86.4 0.8 copy.12
  87.2 0.0 copy-done
  87.2 1.1 %copy.13 = f32[1,1,21,128,128]{4,3,2,1,0:T(8,128)} copy(f32[1,1,21,128,128]{4,3,2,1,0:T(8,128)S(1)} %bitcast.2) | data formatting | bytes 2752512
  (3 shorter events, 0.0 us)
Async XLA Ops:
  83.9 2.5 %copy-start.1 = (bf16[256,896]{1,0:T(8,128)(2,1)S(1)}, bf16[256,896]{1,0:T(8,128)(2,1)}, u32[]{:S(2)}) copy-start(bf16[256,896]{1,0:T(8,128)(2,1)} %get-tuple-element.15) | copy-start | bytes 1376260
  83.9 3.2 %copy-start = (f32[21,128,128]{2,1,0:T(8,128)S(1)}, f32[21,128,128]{2,1,0:T(8,128)}, u32[]{:S(2)}) copy-start(f32[21,128,128]{2,1,0:T(8,128)} %get-tuple-element.8) | copy-start | bytes 4128772

commit v3 on v2

--- a/solution.py
+++ b/solution.py
@@ -147,22 +147,35 @@
         return (z + 1 + j <= last,
                 copy(piece, piece, yl_sem.at[0, j, b], yl_sem.at[1, j, b], y_dev))
 
-    def y_x(part):
-        piece = part(z * 2 + 1 - x)
-        return (None, copy(piece, piece, yx_sem.at[0], yx_sem.at[1], y_dev))
+    def third(side, owner, sub):
+        return wbuf.at[side, pl.ds(owner * capacity + sub * part, part)]
+
+    def y_x(side, sub):
+        piece = third(side, z * 2 + 1 - x, sub)
+        return copy(piece, piece, yx_sem.at[0, sub], yx_sem.at[1, sub], y_dev)
 
     mine = store_hbm.at[:, pl.ds(pl.multiple_of(group * half, half), half), :]
 
     def from_store(cond, sems, device):
         start(cond, copy(mine, chunk(me), sems[0], sems[1], device))
 
-    from_store(None, (ax_sem.at[0], ax_sem.at[1]), x_dev)
+    for sub in range(subs):
+        start(None, copy(mine.at[sub * part:(sub + 1) * part], third(group, me, sub),
+                         ax_sem.at[0, sub], ax_sem.at[1, sub], x_dev))
     if paired:
         start(None, copy(grad_hbm, gfull.at[core], g_sem.at[0], g_sem.at[1], core_dev))
     from_store(z < last, (ar_sem.at[0, 0, 0], ar_sem.at[1, 0, 0]), up_dev)
     from_store(z > 0, (al_sem.at[0, 0, 0], al_sem.at[1, 0, 0]), down_dev)
     for desc in store_in:
         desc.start()
+
+    def gather_x(sub):
+        piece = third(group, z * 2 + 1 - x, sub)
+        copy(piece, piece, ax_sem.at[0, sub], ax_sem.at[1, sub], x_dev).wait_recv()
+        start(None, y_x(group, sub))
+        if sub == subs - 1:
+            start(*up_send(0, 1))
+            start(*down_send(0, 1))
 
     hid_in.wait()
     for r in range(row_tiles):
@@ -210,13 +223,6 @@
             value = jnp.where(z == at, order[k], value)
         return value
 
-    def gather_x():
-        part = chunk(z * 2 + 1 - x)
-        copy(part, part, ax_sem.at[0], ax_sem.at[1], x_dev).wait_recv()
-        start(*up_send(0, 1))
-        start(*down_send(0, 1))
-        start(*y_x(chunk))
-
     def gather_z(j, b):
         wait_recv(*up_recv(j, b))
         if j + 1 < last:
@@ -227,7 +233,7 @@
             start(*down_send(j + 1, b))
         start(*y_down(j, b, chunk))
 
-    steps = [gather_x]
+    steps = [functools.partial(gather_x, sub) for sub in range(subs)]
     for j in range(last):
         for b in range(2):
             steps.append(functools.partial(gather_z, j, b))
@@ -249,12 +255,10 @@
         for sub in range(subs):
             pieces(targets[k] * 2 + 1 - x, sub)
             start(None, x_copy(k, sub))
-        if k == 0:
-            gather_step()
     for k in range(lines):
         for sub in range(subs):
             pieces(targets[k] * 2 + x, sub)
-        if k == 0:
+        if k < subs:
             gather_step()
 
     def arrived(slot, k, sub):
@@ -319,15 +323,15 @@
 
     for k in range(last):
         for sub in range(subs):
+            gather_step()
             add_up(k, sub)
-            if sub % 2 == 0:
-                gather_step()
     for step in steps:
         step()
 
     for desc in store_in:
         desc.wait()
-    wait_recv(*y_x(other_chunk))
+    for sub in range(subs):
+        y_x(1 - group, sub).wait_recv()
     for j in range(last):
         for b in range(2):
             wait_recv(*y_up(j, b, other_chunk))
@@ -432,8 +436,8 @@
             pltpu.VMEM((few, tokens, 2 * width), bf16),
             pltpu.VMEM((few, tokens, 2 * width), bf16),
             pltpu.VMEM((few, tokens, 2 * width), bf16),
-            dma((4,)), dma((2,)), dma((2,)), dma((2, hops, 2)), dma((2, hops, 2)),
-            dma((2,)), dma((2, hops, 2)), dma((2, hops, 2)),
+            dma((4,)), dma((2,)), dma((2, subs)), dma((2, hops, 2)), dma((2, hops, 2)),
+            dma((2, subs)), dma((2, hops, 2)), dma((2, hops, 2)),
             dma((2, lines * subs)), dma((lines, subs)), dma((lines + 1, subs)), dma((2, few)),
         ],
         compiler_params=pltpu.CompilerParams(

time: 88.5 us -> 84.7 us (0.957)
  Pallas kernels: 79.1 us -> 75.3 us
    pallas_call x1, Pallas kernels: 79.1 us -> 75.3 us  [shards(): pl.pallas_call(functools.partial(kernel, cfg), out_shape=(jax.ShapeDtypeS...]
where the time goes in v3:
time: 84.7 us; the launch traced here: 84.4 us
  Pallas kernels  75.3 us (89%)
  local copies, waits for them, and re-layouts  5.99 us (7%)
  other arithmetic  2.45 us (3%)
    pallas_call x1, Pallas kernels, shards(): pl.pallas_call(functools.partial(kernel, cfg), out_shape=(jax.ShapeDtypeS...  75.3 us
    unnamed x7, local copies, waits for them, and re-layouts  4.29 us

profile of v3, /device:TPU:0, one launch (start us, length us, event | category | flops | bytes accessed | tf_op | source)
XLA Modules:
  0.0 84.4 jit_solution(6173299904134532566)
XLA Ops:
  0.6 0.8 reshape.58
  1.4 0.2 convert_reduce_fusion
  1.6 0.8 reshape.59
  2.4 0.1 select_reduce_fusion
  2.5 0.1 reduce_sum.31
  2.6 0.7 add_add_fusion
  3.3 0.8 select_reduce_fusion.1
  4.1 0.1 add.53
  4.1 0.7 pad_add_fusion.tab
  4.8 75.3 %shard_map.76 = (bf16[256,2048]{1,0:T(8,128)(2,1)}, bf16[256,896]{1,0:T(8,128)(2,1)}, f32[21,128,128]{2,1,0:T(8,128)}) custom-call(s32[392]{0:T(512)} %pad_add_fusion.tab, bf16[256,896]{1,0:T(8,128)(2,1)} %hid_hbm.1, bf16[256,2048]{1,0:T(8,128)(2,1)} %grad_hbm.1, bf16[21,128,128]{2,1,0:T(8,128)(2,1)} %bitcast.3), custom_call_target="tpu_custom_call" | custom-call | tf_op jit(solution)/shard_map/pallas_call | solution.py:416
  80.1 0.0 copy-start.1
  80.1 0.0 copy-start
  80.1 2.4 %copy.11 = bf16[256,2048]{1,0:T(8,128)(2,1)} copy(bf16[256,2048]{1,0:T(8,128)(2,1)} %get-tuple-element.14) | data formatting | bytes 2097152
  82.6 0.0 copy-done.1
  82.6 0.8 copy.12
  83.3 0.0 copy-done
  83.3 1.1 %copy.13 = f32[1,1,21,128,128]{4,3,2,1,0:T(8,128)} copy(f32[1,1,21,128,128]{4,3,2,1,0:T(8,128)S(1)} %bitcast.2) | data formatting | bytes 2752512
  (3 shorter events, 0.0 us)
Async XLA Ops:
  80.1 2.5 %copy-start.1 = (bf16[256,896]{1,0:T(8,128)(2,1)S(1)}, bf16[256,896]{1,0:T(8,128)(2,1)}, u32[]{:S(2)}) copy-start(bf16[256,896]{1,0:T(8,128)(2,1)} %get-tuple-element.15) | copy-start | bytes 1376260
  80.1 3.2 %copy-start = (f32[21,128,128]{2,1,0:T(8,128)S(1)}, f32[21,128,128]{2,1,0:T(8,128)}, u32[]{:S(2)}) copy-start(f32[21,128,128]{2,1,0:T(8,128)} %get-tuple-element.8) | copy-start | bytes 4128772
